TPU v7x, 512 devices: a whole 4x8x8 slice. The times are simulated.
512 devices in a mesh: shot: 32 (over y_lo, x, core), pair: 16 (over y_hi, z).
Axes of the slice: x: 4, y: 8 (y_hi: 2, y_lo: 4; y = y_hi * 4 + y_lo), z: 8, core: 2. Of those that a mesh axis runs over, the one named last changes fastest.
Arguments:
- spectra: bfloat16 [2, 512, 128, 1024], P(None, 'shot', None, 'pair'), may hold values from -6 to 6
- shot_weight: float32 [512], P('shot'), may hold values from 0.5 to 2
Outputs:
- virtual_gather: bfloat16 [2, 128, 1024, 1024], P(None, 'shot', 'pair')
All inputs are finite; a program needn't handle non-finite values.
Results may differ from a plain program's by a relative error of at most 0.0054.
Values may be sent and summed in bfloat16 or wider, within the bound.
No kernel may reach another device: no remote copies, remote signals or barrier semaphores. Data moves between devices by JAX's collectives and lax.ppermute only.
A program may use at most 64 MiB of HBM per device.

v0:
```python
import jax
import jax.numpy as jnp
from jax import lax
from jax.sharding import PartitionSpec as P


def gram_block(row_data, column_data, factor):
    swapped = jnp.stack([-row_data[1], row_data[0]])
    left_side = jnp.stack([row_data, swapped])
    product = jnp.einsum(
        "ocsfa,csfb->ofab", left_side, column_data, preferred_element_type=jnp.float32
    )
    return product * factor


def shards(spectra, shot_weight):
    scaled = (spectra.astype(jnp.float32) * shot_weight[None, :, None, None]).astype(jnp.bfloat16)
    by_freq = lax.all_to_all(scaled, "shot", split_axis=2, concat_axis=1, tiled=True)
    total_shots = by_freq.shape[1]
    factor = total_shots ** (-0.5)
    local_bins = by_freq.shape[2]
    row_width = by_freq.shape[3]
    gathered = lax.all_gather(by_freq, "pair", axis=3, tiled=True)
    device_count = lax.axis_size("pair")
    own_index = lax.axis_index("pair")

    def one_tile(tile_index):
        columns = lax.dynamic_slice_in_dim(gathered, tile_index * row_width, row_width, 3)
        return lax.cond(
            tile_index >= own_index,
            lambda: gram_block(by_freq, columns, factor).astype(jnp.bfloat16),
            lambda: jnp.zeros((2, local_bins, row_width, row_width), jnp.bfloat16),
        )

    tiles = lax.map(one_tile, jnp.arange(device_count, dtype=jnp.int32))
    received = lax.all_to_all(tiles, "pair", split_axis=0, concat_axis=0, tiled=True)
    mirrored = jnp.stack(
        [jnp.swapaxes(received[:, 0], 2, 3), -jnp.swapaxes(received[:, 1], 2, 3)], axis=1
    )
    below_diag = (jnp.arange(device_count, dtype=jnp.int32) < own_index)[:, None, None, None, None]
    merged = jnp.where(below_diag, mirrored, tiles)
    return merged.transpose(1, 2, 3, 0, 4).reshape(
        2, local_bins, row_width, device_count * row_width
    )


def solution(mesh):
    return jax.shard_map(
        shards,
        mesh=mesh,
        in_specs=(P(None, "shot", None, "pair"), P("shot")),
        out_specs=P(None, "shot", "pair", None),
        check_vma=False,
    )
```

profile of v0, /device:TPU:16, one launch (start us, length us, event | category | flops | bytes accessed | tf_op | source)
XLA Modules:
  0.0 356.7 jit_solution(6008609927738838939)
XLA Ops:
  10.1 23.1 %all_to_all.23 = bf16[32,2,4096]{2,1,0:T(2,128)(2,1)S(1)} all-to-all(bf16[32,2,4096]{2,1,0:T(2,128)(2,1)S(1)} %reshape.12), channel_id=1, replica_groups=mesh['shot'=32,'pair'=16] {'shot'}, dimensions={0} | all-to-all | bytes 1048576 | tf_op jit(solution)/shard_map/all_to_all | solution.py:18
  35.8 194.2 %all-gather.2.cloned.1.call-done = bf16[2,512,4,1024]{1,2,0,3:T(4,128)(2,1)} async-done(((bf16[2,512,4,64]{1,2,0,3:T(4,128)(2,1)}), bf16[2,512,4,1024]{1,2,0,3:T(4,128)(2,1)}) %all-gather.2.cloned.1.call-update) | async-done | bytes 8388624 | tf_op jit(solution)/shard_map/all_gather | solution.py:23
  230.0 9.5 %copy.38 = bf16[2,512,4,1024]{1,3,0,2:T(8,128)(2,1)} copy(bf16[2,512,4,1024]{1,2,0,3:T(4,128)(2,1)} %all-gather.2.cloned.1.call-done) | data formatting | bytes 16777216 | tf_op jit(solution)/shard_map/while | solution.py:35
  239.5 56.6 %while.10 = (s32[]{:T(128)}, bf16[16,2,4,64,64]{4,3,1,2,0:T(8,128)(2,1)S(1)}, s32[16]{0:T(128)S(1)}, s32[]{:T(128)}, bf16[2,512,4,64]{1,3,0,2:T(8,128)(2,1)S(1)}, /*index=5*/bf16[2,512,4,1024]{1,3,0,2:T(8,128)(2,1)}, s32[]{:T(128)}) while((s32[]{:T(128)}, bf16[16,2,4,64,64]{4,3,1,2,0:T(8,128)(2,1)S(1)}, s32[16]{0:T(128)S(1)}, s32[]{:T(128)}, ...), condition=%wide.region_3.4_spmd, body=%wide.region_0.3_spmd.sunk | while | flops 68091904 | bytes 3997893 | solution.py:35
  240.7 2.2 conditional.2
  244.3 2.2 conditional.2
  247.8 2.2 conditional.2
  251.4 2.2 conditional.2
  254.9 2.2 conditional.2
  262.0 2.2 conditional.2
  265.5 2.2 conditional.2
  269.1 2.2 conditional.2
  272.6 2.2 conditional.2
  276.1 2.2 conditional.2
  279.7 2.2 conditional.2
  283.2 2.2 conditional.2
  286.8 2.2 conditional.2
  293.8 2.2 conditional.2
  296.1 2.6 copy.39
  298.7 4.6 %reshape.14 = bf16[16,2,16384]{2,1,0:T(2,128)(2,1)} reshape(bf16[16,2,4,64,64]{4,3,2,1,0:T(8,128)(2,1)} %bitcast.54) | data formatting | bytes 2097152
  303.4 4.5 %all-to-all-start.1 = ((bf16[16,2,16384]{2,1,0:T(2,128)(2,1)}), bf16[16,2,16384]{2,1,0:T(2,128)(2,1)}, u32[]{:S(2)}, u32[]{:S(2)}) async-start(bf16[16,2,16384]{2,1,0:T(2,128)(2,1)} %reshape.14), calls=%async_computation.1 | async-start | bytes 2097152 | tf_op jit(solution)/shard_map/all_to_all | solution.py:36
  307.9 31.3 %all-to-all-done.1 = bf16[16,2,16384]{2,1,0:T(2,128)(2,1)} async-done(((bf16[16,2,16384]{2,1,0:T(2,128)(2,1)}), bf16[16,2,16384]{2,1,0:T(2,128)(2,1)}, u32[]{:S(2)}, u32[]{:S(2)}) %all-to-all-start.1) | async-done | bytes 1048608 | tf_op jit(solution)/shard_map/all_to_all | solution.py:36
  339.2 4.7 %reshape.15 = bf16[16,2,4,64,64]{4,3,2,1,0:T(8,128)(2,1)} reshape(bf16[16,2,16384]{2,1,0:T(2,128)(2,1)} %all-to-all-done.1) | data formatting | bytes 2097152
  347.6 2.3 reshape.9
  (99 shorter events, 49.0 us)
Async XLA Ops:
  6.5 223.5 %all-gather.2.cloned.1.call-start = ((), (), s32[]{:S(2)}) async-start(), calls=%async_computation.2 | async-start | bytes 8912896 | tf_op jit(solution)/shard_map/all_gather | solution.py:23
  35.8 203.7 %copy-start = (bf16[16,2,4,64,64]{4,3,1,2,0:T(8,128)(2,1)S(1)}, bf16[16,2,4,64,64]{4,3,1,2,0:T(8,128)(2,1)}, u32[]{:S(2)}) copy-start(bf16[16,2,4,64,64]{4,3,1,2,0:T(8,128)(2,1)} %custom-call) | copy-start | bytes 3145732
  303.4 35.8 %all-to-all-start.1 = ((bf16[16,2,16384]{2,1,0:T(2,128)(2,1)}), bf16[16,2,16384]{2,1,0:T(2,128)(2,1)}, u32[]{:S(2)}, u32[]{:S(2)}) async-start(bf16[16,2,16384]{2,1,0:T(2,128)(2,1)} %reshape.14), calls=%async_computation.1 | async-start | bytes 2097152 | tf_op jit(solution)/shard_map/all_to_all | solution.py:36
Sparse Core Ops, SparseCore 0:
  35.6 194.4 all-gather.1
where the time goes:
time: 358 us; the launch traced here: 357 us
  waiting for transfers between devices  226 us (63%)
  local copies, waits for them, and re-layouts  39.7 us (11%)
  matrix products  23.5 us (7%)
  blocking collectives  23.1 us (6%)
  loops' own time  21.9 us (6%)
  between operations  13.5 us (4%)
  other arithmetic  4.96 us (1%)
  starting transfers between devices  4.54 us (1%)
    all_gather x1, waiting for transfers between devices, shards(): gathered = lax.all_gather(by_freq, 'pair', axis=3, tiled=True)  194 us
    all_to_all x1, waiting for transfers between devices, shards(): lax.all_to_all(tiles, 'pair', split_axis=0, concat_axis=0, tiled=True)  31.3 us
    dot_general x16, matrix products, gram_block(): jnp.einsum('ocsfa,csfb->ofab', left_side, column_data, preferred_element_...  23.5 us
    all_to_all x1, blocking collectives, shards(): lax.all_to_all(scaled, 'shot', split_axis=2, concat_axis=1, tiled=True)  23.1 us
    while x3, local copies, waits for them, and re-layouts, shards(): tiles = lax.map(one_tile, jnp.arange(device_count, dtype=jnp.int32))  12.4 us
    another operation x16, loops' own time, one_tile(): lax.cond(tile_index >= own_index, lambda: gram_block(by_freq, columns, fa...  11 us
    another operation x1, loops' own time, shards(): tiles = lax.map(one_tile, jnp.arange(device_count, dtype=jnp.int32))  10.9 us
    unnamed x6, local copies, waits for them, and re-layouts  10.7 us
  transfers between devices with their start and end apart: 2, of which 2 were waited for; matrix products, arithmetic and copies ran while one was open for 0% of the time, Pallas kernels for 0%

commit v1 on v0

--- a/solution.py
+++ b/solution.py
@@ -20,7 +20,8 @@
     factor = total_shots ** (-0.5)
     local_bins = by_freq.shape[2]
     row_width = by_freq.shape[3]
-    gathered = lax.all_gather(by_freq, "pair", axis=3, tiled=True)
+    outgoing = jnp.stack([by_freq] * lax.axis_size("pair"))
+    gathered = jnp.concatenate(lax.all_to_all(outgoing, "pair", 0, 0), axis=3)
     device_count = lax.axis_size("pair")
     own_index = lax.axis_index("pair")
 

time: 358 us -> 495 us (1.38)
  the two profiles are of different devices: /device:TPU:16 before, /device:TPU:112 now
where the time goes in v1:
time: 495 us; the launch traced here: 494 us
  waiting for transfers between devices  349 us (71%)
  local copies, waits for them, and re-layouts  46.4 us (9%)
  starting transfers between devices  46.3 us (9%)
  blocking collectives  21.5 us (4%)
  loops' own time  15.5 us (3%)
  matrix products  10.3 us (2%)
    all_to_all x1, waiting for transfers between devices, shards(): gathered = jnp.concatenate(lax.all_to_all(outgoing, 'pair', 0, 0), axis=3)  322 us
    all_to_all x1, starting transfers between devices, shards(): lax.all_to_all(tiles, 'pair', split_axis=0, concat_axis=0, tiled=True)  31.5 us
    all_to_all x1, waiting for transfers between devices, shards(): lax.all_to_all(tiles, 'pair', split_axis=0, concat_axis=0, tiled=True)  26.8 us
    all_to_all x1, blocking collectives, shards(): lax.all_to_all(scaled, 'shot', split_axis=2, concat_axis=1, tiled=True)  21.5 us
    all_to_all x1, starting transfers between devices, shards(): gathered = jnp.concatenate(lax.all_to_all(outgoing, 'pair', 0, 0), axis=3)  14.8 us
    another operation x1, loops' own time, shards(): tiles = lax.map(one_tile, jnp.arange(device_count, dtype=jnp.int32))  10.7 us
    dot_general x7, matrix products, gram_block(): jnp.einsum('ocsfa,csfb->ofab', left_side, column_data, preferred_element_...  10.3 us
    while x3, local copies, waits for them, and re-layouts, shards(): tiles = lax.map(one_tile, jnp.arange(device_count, dtype=jnp.int32))  10.1 us
  transfers between devices with their start and end apart: 2, of which 2 were waited for; matrix products, arithmetic and copies ran while one was open for 0% of the time, Pallas kernels for 0%

profile of v1, /device:TPU:112, one launch (start us, length us, event | category | flops | bytes accessed | tf_op | source)
XLA Modules:
  0.0 493.5 jit_solution(3526894565201540518)
XLA Ops:
  1.2 1.6 copy.33
  3.6 21.5 %all_to_all.25 = bf16[32,2,4096]{2,1,0:T(2,128)(2,1)S(1)} all-to-all(bf16[32,2,4096]{2,1,0:T(2,128)(2,1)S(1)} %reshape.23), channel_id=1, replica_groups=mesh['shot'=32,'pair'=16] {'shot'}, dimensions={0} | all-to-all | bytes 1048576 | tf_op jit(solution)/shard_map/all_to_all | solution.py:18
  26.3 4.3 stack.52
  30.6 14.8 %all-to-all-start.1 = ((bf16[16,2,512,4,64]{2,4,1,3,0:T(8,128)(2,1)}), bf16[16,2,512,4,64]{2,4,1,3,0:T(8,128)(2,1)}, u32[]{:S(2)}, u32[]{:S(2)}) async-start(bf16[16,2,512,4,64]{2,4,1,3,0:T(8,128)(2,1)} %stack.52), calls=%async_computation.1 | async-start | bytes 16777216 | tf_op jit(solution)/shard_map/all_to_all | solution.py:24
  45.4 322.4 %all-to-all-done.1 = bf16[16,2,512,4,64]{2,4,1,3,0:T(8,128)(2,1)} async-done(((bf16[16,2,512,4,64]{2,4,1,3,0:T(8,128)(2,1)}), bf16[16,2,512,4,64]{2,4,1,3,0:T(8,128)(2,1)}, u32[]{:S(2)}, u32[]{:S(2)}) %all-to-all-start.1) | async-done | bytes 8388640 | tf_op jit(solution)/shard_map/all_to_all | solution.py:24
  367.8 7.7 %copy.37 = bf16[16,2,512,4,64]{2,4,0,3,1:T(8,128)(2,1)} copy(bf16[16,2,512,4,64]{2,4,1,3,0:T(8,128)(2,1)} %all-to-all-done.1) | data formatting | bytes 16777216 | tf_op jit(solution)/shard_map/all_to_all | solution.py:24
  375.5 7.2 %copy.39 = bf16[2,512,4,1024]{1,3,0,2:T(8,128)(2,1)} copy(bf16[2,512,4,1024]{1,3,2,0:T(8,128)(2,1)} %bitcast.53) | data formatting | bytes 16777216 | tf_op jit(solution)/shard_map/while | solution.py:36
  382.6 36.9 %while.10 = (s32[]{:T(128)}, bf16[16,2,4,64,64]{4,3,1,2,0:T(8,128)(2,1)S(1)}, s32[16]{0:T(128)S(1)}, s32[]{:T(128)}, bf16[2,512,4,64]{1,3,0,2:T(8,128)(2,1)S(1)}, /*index=5*/bf16[2,512,4,1024]{1,3,0,2:T(8,128)(2,1)}, s32[]{:T(128)}) while((s32[]{:T(128)}, bf16[16,2,4,64,64]{4,3,1,2,0:T(8,128)(2,1)S(1)}, s32[16]{0:T(128)S(1)}, s32[]{:T(128)}, ...), condition=%wide.region_3.4_spmd, body=%wide.region_0.3_spmd.sunk | while | flops 68091904 | bytes 3997885 | solution.py:36
  396.1 2.2 conditional.2
  396.8 1.5 fusion.2
  399.6 2.2 conditional.2
  400.4 1.5 fusion.2
  403.1 2.2 conditional.2
  406.7 2.2 conditional.2
  410.2 2.2 conditional.2
  413.7 2.2 conditional.2
  417.3 2.2 conditional.2
  419.6 2.6 copy.40
  422.2 4.6 reshape.25
  426.8 31.5 %all-to-all-start.2 = ((bf16[16,2,16384]{2,1,0:T(2,128)(2,1)}), bf16[16,2,16384]{2,1,0:T(2,128)(2,1)S(1)}, u32[]{:S(2)}, u32[]{:S(2)}) async-start(bf16[16,2,16384]{2,1,0:T(2,128)(2,1)} %reshape.25), calls=%async_computation.2 | async-start | bytes 2097152 | tf_op jit(solution)/shard_map/all_to_all | solution.py:37
  458.4 26.8 %all-to-all-done.2 = bf16[16,2,16384]{2,1,0:T(2,128)(2,1)S(1)} async-done(((bf16[16,2,16384]{2,1,0:T(2,128)(2,1)}), bf16[16,2,16384]{2,1,0:T(2,128)(2,1)S(1)}, u32[]{:S(2)}, u32[]{:S(2)}) %all-to-all-start.2) | async-done | bytes 1048608 | tf_op jit(solution)/shard_map/all_to_all | solution.py:37
  485.2 2.4 reshape.26
  487.5 1.7 slice_bitcast_fusion
  491.2 2.3 reshape.20
  (79 shorter events, 23.9 us)
Async XLA Ops:
  30.6 337.2 %all-to-all-start.1 = ((bf16[16,2,512,4,64]{2,4,1,3,0:T(8,128)(2,1)}), bf16[16,2,512,4,64]{2,4,1,3,0:T(8,128)(2,1)}, u32[]{:S(2)}, u32[]{:S(2)}) async-start(bf16[16,2,512,4,64]{2,4,1,3,0:T(8,128)(2,1)} %stack.52), calls=%async_computation.1 | async-start | bytes 16777216 | tf_op jit(solution)/shard_map/all_to_all | solution.py:24
  426.8 58.4 %all-to-all-start.2 = ((bf16[16,2,16384]{2,1,0:T(2,128)(2,1)}), bf16[16,2,16384]{2,1,0:T(2,128)(2,1)S(1)}, u32[]{:S(2)}, u32[]{:S(2)}) async-start(bf16[16,2,16384]{2,1,0:T(2,128)(2,1)} %reshape.25), calls=%async_computation.2 | async-start | bytes 2097152 | tf_op jit(solution)/shard_map/all_to_all | solution.py:37
